TPU v7x, 32 devices: a whole 2x2x4 slice. The times are simulated.
32 devices in a mesh: groups: 2 (over x), pool: 16 (over z, y, core).
Axes of the slice: x: 2, y: 2, z: 4, core: 2. Of those that a mesh axis runs over, the one named last changes fastest.
Arguments:
- queries: bfloat16 [1024, 16384], P(None, ('groups', 'pool')), parts along dimension 1, may hold values from -80 to 80
- stretch_keys: bfloat16 [16384, 128], P(('groups', 'pool')), parts along dimension 0, may hold values from -6 to 6
- stretch_values: bfloat16 [16384, 128], P(('groups', 'pool')), parts along dimension 0, may hold values from -6 to 6
- pool_keys: bfloat16 [96, 256, 128], P(('groups', 'pool')), parts along dimension 0, may hold values from -8 to 8
- pool_values: bfloat16 [96, 256, 128], P(('groups', 'pool')), parts along dimension 0, may hold values from -6 to 6
- page_counts: int32 [4], P('groups'), parts along dimension 0, may hold values from 1 to 11, as said below
- page_table: int32 [4, 4, 11], P('groups'), parts along dimension 0, may hold values from -1 to 47, as said below
Outputs:
- attended: bfloat16 [1024, 16384], P(None, ('groups', 'pool')), parts along dimension 1
There are 2 independent parts, one for each index of `groups`. A program takes and returns all parts, laid end to end along the dimension named above; each array names one. Nothing has to cross between parts.
Inputs may be any that keep to these rules, and one draw needn't show every extreme that they name: `page_counts`: the counts sum to 12; the largest is exactly 11. `page_table`: entry [r, g, j] with j < page_counts[r] is the slot of pool_keys and pool_values holding page j of request r for key head g; slot s lies on device s // 3 of the pool axis. Other entries are -1. Every slot is named exactly once. No device holds two slots named by the same r and g.
All inputs are finite; a program needn't handle non-finite values.
Results may differ from a plain program's by a relative error of at most 0.0055.
Values may be sent and summed in bfloat16 or wider, within the bound.
No kernel may reach another device: no remote copies, remote signals or barrier semaphores. Data moves between devices by JAX's collectives and lax.ppermute only.
A program may use at most 64 MiB of HBM per device.

v0:
```python
import functools
import math

import jax
import jax.numpy as jnp
from jax import lax
from jax.experimental import pallas as pl
from jax.experimental.pallas import tpu as pltpu
from jax.sharding import PartitionSpec as P

HD = 128
QH = 32
KVH = 4
PAGE = 256
STRETCH = 1024
SLOTS_DEV = 3
CORES = 2
TILE = 256
VMEM_BYTES = 24 * 2**20
PICK_VMEM = 56 * 2**20
BLOCK = 4
WAVES = 2
HEAD = WAVES + 1
EXP2_SCALE = math.log2(math.e) / math.sqrt(HD)
ROW_BY_ROW = (((1,), (1,)), ((), ()))

VMEM = pl.BlockSpec(memory_space=pltpu.VMEM)
SMEM = pl.BlockSpec(memory_space=pltpu.SMEM)
ANY = pl.BlockSpec(memory_space=pl.ANY)
DONE = jax.ShapeDtypeStruct((8, HD), jnp.float32)


def swapped(value, axis, mask):
    pairs = [(source, source ^ mask) for source in range(lax.axis_size(axis))]
    return lax.ppermute(value, axis, pairs)


def pick_kernel(offsets, own_ref, table_ref, keys_ref, values_ref, new_keys_ref, new_values_ref, *refs):
    *outs, new_out, held, new_held, sem, sent = refs
    loads = [
        pltpu.make_async_copy(source, held.at[side], sem.at[side])
        for side, source in enumerate((keys_ref, values_ref))
    ]
    loads += [
        pltpu.make_async_copy(source, new_held.at[side], sem.at[2 + side])
        for side, source in enumerate((new_keys_ref, new_values_ref))
    ]
    for copy in loads:
        copy.start()
    own = own_ref[0]
    first = own * SLOTS_DEV
    key_heads, depth = table_ref.shape[1:]
    slots = []
    for offset in offsets:
        row = jnp.bitwise_xor(own // CORES, offset)

        def look(page, slot, row=row):
            there = table_ref[row // key_heads, row % key_heads, page] - first
            return jnp.where((there >= 0) & (there < SLOTS_DEV), there, slot)

        slots.append(lax.fori_loop(0, depth, look, 0, unroll=True))
    for copy in loads:
        copy.wait()
    stores = [
        pltpu.make_async_copy(held.at[side, slot], out.at[side], sent.at[at, side])
        for at, (out, slot) in enumerate(zip(outs, slots))
        for side in range(2)
    ]
    stores.append(pltpu.make_async_copy(new_held, new_out, sent.at[len(offsets), 0]))
    for copy in stores:
        copy.start()
    for copy in stores:
        copy.wait()


def pick(own, table, keys, values, new_keys, new_values, offsets):
    return pl.pallas_call(
        functools.partial(pick_kernel, offsets),
        out_shape=[jax.ShapeDtypeStruct((2, PAGE, HD), keys.dtype)] * len(offsets)
        + [jax.ShapeDtypeStruct((2,) + new_keys.shape, new_keys.dtype)],
        in_specs=[SMEM, SMEM] + [ANY] * 4,
        out_specs=[ANY] * (len(offsets) + 1),
        scratch_shapes=[
            pltpu.VMEM((2,) + keys.shape, keys.dtype),
            pltpu.VMEM((2,) + new_keys.shape, new_keys.dtype),
            pltpu.SemaphoreType.DMA((4,)),
            pltpu.SemaphoreType.DMA((len(offsets) + 1, 2)),
        ],
        compiler_params=pltpu.CompilerParams(vmem_limit_bytes=PICK_VMEM),
        name="pick",
    )(own, table, keys, values, new_keys, new_values)


def pack_kernel(count, *refs):
    for at in range(count):
        refs[-1][at] = refs[at][...]


def pack(arrays, after):
    count = len(arrays)
    return pl.pallas_call(
        functools.partial(pack_kernel, count),
        out_shape=jax.ShapeDtypeStruct((count,) + arrays[0].shape, arrays[0].dtype),
        in_specs=[VMEM] * count + [ANY] * len(after),
        out_specs=VMEM,
        compiler_params=pltpu.CompilerParams(vmem_limit_bytes=VMEM_BYTES),
        name="pack",
    )(*arrays, *after)


def online(scores, values, old_max, old_totals, old_acc, shares=None):
    width = scores.shape[1] // HD
    peak = jnp.max(scores, axis=1, keepdims=True)
    new_max = jnp.broadcast_to(peak, (scores.shape[0], HD))
    if old_max is not None:
        new_max = jnp.maximum(old_max, new_max)
    weights = jnp.exp2((scores - jnp.concatenate([new_max] * width, 1)) * EXP2_SCALE)
    parts = [weights[:, part * HD : (part + 1) * HD] for part in range(width)]
    if shares is not None:
        each = width // len(shares)
        parts = [sum(parts[at * each + 1 : (at + 1) * each], parts[at * each]) for at in range(len(shares))]
        parts = parts[:1] + [part * share for part, share in zip(parts[1:], shares[1:])]
    totals = sum(parts[1:], parts[0])
    acc = jnp.dot(weights.astype(jnp.bfloat16), values, preferred_element_type=jnp.float32)
    if old_max is not None:
        rescale = jnp.exp2((old_max - new_max) * EXP2_SCALE)
        totals = old_totals * rescale + totals
        acc = old_acc * rescale + acc
    return new_max, totals, acc


def score(query, keys):
    return lax.dot_general(query, keys, ROW_BY_ROW, preferred_element_type=jnp.float32)


def list_pages(cuts, own, table_ref, list_ref):
    chip, core = own // CORES, own % CORES
    key_heads, depth = table_ref.shape[1:]
    seen = 0
    for wave in range(WAVES):

        def look(page, seen, wave=wave):
            slot = table_ref[chip // key_heads, chip % key_heads, page]
            device = jnp.maximum(slot, 0) // SLOTS_DEV
            offset = jnp.bitwise_xor(device // CORES, chip)
            inside = (slot >= 0) & (offset >= cuts[wave]) & (offset < cuts[wave + 1])

            @pl.when(inside)
            def _():
                list_ref[HEAD + seen] = (cuts[wave + 1] - 1 - offset) * 2 + jnp.bitwise_xor(device % CORES, core)

            return seen + inside.astype(jnp.int32)

        seen = lax.fori_loop(0, depth, look, seen)
        list_ref[wave] = seen
    early = list_ref[WAVES - 2]
    late = seen - early
    rest = early % BLOCK
    more = (rest + late + BLOCK - 1) // BLOCK > (late + BLOCK - 1) // BLOCK
    list_ref[WAVES] = jnp.where(more, early, early - rest)


def stretch_kernel(cuts, own_ref, table_ref, q_ref, own_kv_ref, other_kv_ref, m_ref, l_ref, a_ref, done_ref, list_ref, ks, vs):
    list_pages(cuts, own_ref[0], table_ref, list_ref)
    half = own_ref[0] % CORES
    rows = own_kv_ref.shape[1]
    for place, source in ((half, own_kv_ref), (1 - half, other_kv_ref)):
        for side, target in enumerate((ks, vs)):
            target[pl.ds(pl.multiple_of(place * rows, rows), rows)] = source[side]
    done_ref[...] = jnp.zeros_like(done_ref)

    tiles = STRETCH // TILE
    row = lax.broadcasted_iota(jnp.int32, (TILE, TILE), 0)
    column = lax.broadcasted_iota(jnp.int32, (TILE, TILE), 1)

    def head(h, _):
        columns = pl.ds(pl.multiple_of(h * HD, HD), HD)

        def scores_of(tile):
            here = slice(tile * TILE, (tile + 1) * TILE)
            scores = score(q_ref[here, columns], ks[: (tile + 1) * TILE])
            last = jnp.where(column <= row, scores[:, tile * TILE :], -jnp.inf)
            if tile == 0:
                return last
            return jnp.concatenate([scores[:, : tile * TILE], last], 1)

        ahead = scores_of(tiles - 1)
        for tile in range(tiles)[::-1]:
            scores = ahead
            if tile > 0:
                ahead = scores_of(tile - 1)
            here = slice(tile * TILE, (tile + 1) * TILE)
            m, l, a = online(scores, vs[: (tile + 1) * TILE], None, None, None)
            m_ref[h, here, :] = m
            l_ref[h, here, :] = l
            a_ref[h, here, :] = a
        return 0

    lax.fori_loop(0, q_ref.shape[1] // HD, head, 0)


def pages_kernel(final, list_ref, q_ref, *refs):
    waves = WAVES if final else WAVES - 1
    sources = [(refs[2 * wave], refs[2 * wave + 1]) for wave in range(waves)]
    refs = refs[2 * waves :]
    if final:
        m_ref, l_ref, a_ref, o_ref, ks, vs, ahead_ref, held, sem = refs
    else:
        m_ref, l_ref, a_ref, done_ref, ks, vs, ahead_ref = refs[3:]
        done_ref[...] = jnp.zeros_like(done_ref)
    skipped = list_ref[WAVES] if final else 0
    limit = list_ref[WAVES - 1] if final else list_ref[WAVES]
    for wave, (near_ref, far_ref) in enumerate(sources):
        start = jnp.maximum(list_ref[wave - 1], skipped) if wave > 0 else skipped
        stop = jnp.minimum(list_ref[wave], limit)

        def take(at, _, near_ref=near_ref, far_ref=far_ref):
            place = list_ref[HEAD + at]
            there = place // 2

            @pl.when(place % 2 == 0)
            def _():
                ks[at - skipped] = near_ref[there, 0]
                vs[at - skipped] = near_ref[there, 1]

            @pl.when(place % 2 == 1)
            def _():
                ks[at - skipped] = far_ref[there, 0]
                vs[at - skipped] = far_ref[there, 1]

            return 0

        lax.fori_loop(start, stop, take, 0)

    filled = limit - skipped
    blocks = (filled + BLOCK - 1) // BLOCK

    def blank(at, _):
        ks[at] = ks[at // BLOCK * BLOCK]
        vs[at] = jnp.zeros((PAGE, HD), vs.dtype)
        return 0

    lax.fori_loop(filled, blocks * BLOCK, blank, 0)
    heads = q_ref.shape[1] // HD
    tiles = STRETCH // TILE
    rows = BLOCK * PAGE
    units = [(h, tile) for h in range(heads) for tile in range(tiles)]

    def scores_of(first, h, tile):
        keys = ks[pl.ds(first, BLOCK)].reshape(rows, HD)
        queries = q_ref[tile * TILE : (tile + 1) * TILE, h * HD : (h + 1) * HD]
        return score(queries, keys)

    @pl.when(blocks > 0)
    def _():
        ahead_ref[...] = scores_of(0, 0, 0)

    def block(at, _):
        first = at * BLOCK
        ahead = ahead_ref[...]
        shares = [jnp.where(first + page < filled, 1.0, 0.0) for page in range(BLOCK)]
        for unit, (h, tile) in enumerate(units):
            scores = ahead
            if unit + 1 < len(units):
                ahead = scores_of(first, *units[unit + 1])
            else:
                ahead_ref[...] = scores_of(jnp.minimum(at + 1, blocks - 1) * BLOCK, 0, 0)
            values = vs[pl.ds(first, BLOCK)].reshape(rows, HD)
            here = slice(tile * TILE, (tile + 1) * TILE)
            m, l, a = online(scores, values, m_ref[h, here, :], l_ref[h, here, :], a_ref[h, here, :], shares)
            m_ref[h, here, :] = m
            l_ref[h, here, :] = l
            a_ref[h, here, :] = a
        return 0

    lax.fori_loop(0, blocks, block, 0)

    if final:

        def out(h):
            columns = pl.ds(pl.multiple_of(h * HD, HD), HD)
            return pltpu.make_async_copy(held.at[h], o_ref.at[:, columns], sem.at[h])

        def finish(h, _):
            high = l_ref[h].astype(jnp.bfloat16)
            low = (l_ref[h] - high.astype(jnp.float32)).astype(jnp.bfloat16)
            ones = jnp.ones((2 * HD, HD), jnp.bfloat16)
            totals = jnp.dot(jnp.concatenate([high, low], 1), ones, preferred_element_type=jnp.float32)
            held[h] = (a_ref[h] / totals).astype(o_ref.dtype)
            out(h).start()
            return 0

        def leave(h, _):
            out(h).wait()
            return 0

        lax.fori_loop(0, heads, finish, 0)
        lax.fori_loop(0, heads, leave, 0)


COST = pl.CostEstimate(flops=1000, bytes_accessed=1000, transcendentals=0)


def attend_pages(cuts, final, pages, queries, received, state):
    waves = WAVES if final else WAVES - 1
    most = CORES * cuts[WAVES - 1]
    if final:
        most = BLOCK - 1 + CORES * (cuts[WAVES] - cuts[WAVES - 1])
    most = min(pages.shape[0] - HEAD, most)
    most = -(-most // BLOCK) * BLOCK
    s_shape = jax.ShapeDtypeStruct(state[0].shape, jnp.float32)
    at = 2 + 2 * waves
    heads = state[0].shape[0]
    return pl.pallas_call(
        functools.partial(pages_kernel, final),
        out_shape=jax.ShapeDtypeStruct(queries.shape, queries.dtype) if final else [s_shape] * 3 + [DONE],
        in_specs=[SMEM] + [VMEM] * (4 + 2 * waves),
        out_specs=ANY if final else [VMEM] * 4,
        input_output_aliases={} if final else {at: 0, at + 1: 1, at + 2: 2},
        scratch_shapes=[
            pltpu.VMEM((most, PAGE, HD), jnp.bfloat16),
            pltpu.VMEM((most, PAGE, HD), jnp.bfloat16),
            pltpu.VMEM((TILE, BLOCK * PAGE), jnp.float32),
        ]
        + final * [pltpu.VMEM((heads, STRETCH, HD), queries.dtype), pltpu.SemaphoreType.DMA((heads,))],
        compiler_params=pltpu.CompilerParams(vmem_limit_bytes=VMEM_BYTES),
        cost_estimate=COST,
        name="pages",
    )(pages, queries, *received, *state[:3])


def shards(queries, stretch_keys, stretch_values, pool_keys, pool_values, page_counts, page_table):
    own_index = lax.axis_index("pool")
    heads = queries.shape[1] // HD
    chips = lax.axis_size("pool") // CORES
    own = own_index.astype(jnp.int32).reshape(1)
    cuts = (0, chips * 3 // 4, chips)
    order = list(range(chips // 2, chips)) + list(range(1, chips // 2)) + [0]
    *pages, stretch = pick(own, page_table, pool_keys, pool_values, stretch_keys, stretch_values, order)
    picked = dict(zip(order, pages))
    got = {at: picked[at] if at == 0 else swapped(picked[at], "pool", at * CORES) for at in order}

    other_stretch = swapped(stretch, "pool", 1)
    s_shape = jax.ShapeDtypeStruct((heads, STRETCH, HD), jnp.float32)
    *state, pages = pl.pallas_call(
        functools.partial(stretch_kernel, cuts),
        out_shape=[s_shape] * 3 + [DONE, jax.ShapeDtypeStruct((HEAD + page_table.shape[2],), jnp.int32)],
        in_specs=[SMEM, SMEM] + [VMEM] * 3,
        out_specs=[VMEM] * 4 + [SMEM],
        scratch_shapes=[
            pltpu.VMEM((STRETCH, HD), jnp.bfloat16),
            pltpu.VMEM((STRETCH, HD), jnp.bfloat16),
        ],
        compiler_params=pltpu.CompilerParams(vmem_limit_bytes=VMEM_BYTES),
        cost_estimate=COST,
        name="stretch",
    )(own, page_table, queries, stretch, other_stretch)

    received = []
    after = state[3:]
    for wave in range(WAVES):
        mine = pack([got[at] for at in range(cuts[wave], cuts[wave + 1])[::-1]], after)
        received += [mine, swapped(mine, "pool", 1)]
        after = [mine]
        if wave >= WAVES - 2:
            state = attend_pages(cuts, wave == WAVES - 1, pages, queries, received, state)
            after = state[3:]
    return state


def solution(mesh):
    placed = (
        P(None, ("groups", "pool")),
        P(("groups", "pool"), None),
        P(("groups", "pool"), None),
        P(("groups", "pool"), None, None),
        P(("groups", "pool"), None, None),
        P("groups"),
        P("groups", None, None),
    )
    return jax.shard_map(
        shards, mesh=mesh, in_specs=placed, out_specs=P(None, ("groups", "pool")), check_vma=False
    )
```

profile of v0, /device:TPU:27, one launch (start us, length us, event | category | flops | bytes accessed | tf_op | source)
XLA Modules:
  0.0 49.7 jit_solution(17252483604090680698)
XLA Ops:
  0.0 3.1 %pick.1 = (bf16[2,256,128]{2,1,0:T(8,128)(2,1)}, bf16[2,256,128]{2,1,0:T(8,128)(2,1)}, bf16[2,256,128]{2,1,0:T(8,128)(2,1)}, bf16[2,256,128]{2,1,0:T(8,128)(2,1)...) custom-call(s32[1]{0:T(128)} %bitcast.own_ref, ...), custom_call_target="tpu_custom_call" | custom-call | tf_op jit(solution)/shard_map/pick/pallas_call | solution.py:77
  3.1 0.7 %collective-permute-start = (bf16[2,512,128]{2,1,0:T(8,128)(2,1)}, bf16[2,512,128]{2,1,0:T(8,128)(2,1)S(1)}, u32[]{:S(2)}, u32[]{:S(2)}) collective-permute-start(bf16[2,512,128]{2,1,0:T(8,128)(2,1)} %get-tuple-element.23.own_kv_ref), channel_id=1, source_target_pairs={{0,1},{1,0},{2,3},{3,2},{4,5},{5,4},{6,7},{7,6},{8,9},{9,8},{10,11... | collective-permute-start | bytes 786440 | tf_op jit(solution)/shard_map/ppermute | solution.py:35
  3.9 1.0 %collective-permute-start.1 = (bf16[2,256,128]{2,1,0:T(8,128)(2,1)}, bf16[2,256,128]{2,1,0:T(8,128)(2,1)S(1)}, u32[]{:S(2)}, u32[]{:S(2)}) collective-permute-start(bf16[2,256,128]{2,1,0:T(8,128)(2,1)} %get-tuple-element.25), channel_id=1, source_target_pairs={{0,10},{1,11},{2,8},{3,9},{4,14},{5,15},{6,12},{7,13},{8,2},{9,3},... | collective-permute-start | bytes 393224 | tf_op jit(solution)/shard_map/ppermute | solution.py:35
  4.9 2.3 %collective-permute-start.2 = (bf16[2,256,128]{2,1,0:T(8,128)(2,1)}, bf16[2,256,128]{2,1,0:T(8,128)(2,1)S(1)}, u32[]{:S(2)}, u32[]{:S(2)}) collective-permute-start(bf16[2,256,128]{2,1,0:T(8,128)(2,1)} %get-tuple-element.26), channel_id=1, source_target_pairs={{0,8},{1,9},{2,10},{3,11},{4,12},{5,13},{6,14},{7,15},{8,0},{9,1},... | collective-permute-start | bytes 393224 | tf_op jit(solution)/shard_map/ppermute | solution.py:35
  7.2 0.1 collective-permute-start.3
  7.3 1.3 %collective-permute-start.4 = (bf16[2,256,128]{2,1,0:T(8,128)(2,1)}, bf16[2,256,128]{2,1,0:T(8,128)(2,1)S(1)}, u32[]{:S(2)}, u32[]{:S(2)}) collective-permute-start(bf16[2,256,128]{2,1,0:T(8,128)(2,1)} %get-tuple-element.28), channel_id=1, source_target_pairs={{0,4},{1,5},{2,6},{3,7},{4,0},{5,1},{6,2},{7,3},{8,12},{9,13},{10,... | collective-permute-start | bytes 393224 | tf_op jit(solution)/shard_map/ppermute | solution.py:35
  8.6 0.0 collective-permute-done.other_kv_ref
  8.6 1.2 %collective-permute-start.5 = (bf16[2,256,128]{2,1,0:T(8,128)(2,1)}, bf16[2,256,128]{2,1,0:T(8,128)(2,1)S(1)}, u32[]{:S(2)}, u32[]{:S(2)}) collective-permute-start(bf16[2,256,128]{2,1,0:T(8,128)(2,1)} %get-tuple-element.29), channel_id=1, source_target_pairs={{0,2},{1,3},{2,0},{3,1},{4,6},{5,7},{6,4},{7,5},{8,10},{9,11},{10,... | collective-permute-start | bytes 393224 | tf_op jit(solution)/shard_map/ppermute | solution.py:35
  9.9 1.2 %copy-done = bf16[1024,512]{1,0:T(8,128)(2,1)S(1)} copy-done((bf16[1024,512]{1,0:T(8,128)(2,1)S(1)}, bf16[1024,512]{1,0:T(8,128)(2,1)}, u32[]{:S(2)}) %copy-start) | copy-done | bytes 1048600
  11.1 0.9 %copy-done.2 = bf16[2,512,128]{2,1,0:T(8,128)(2,1)S(1)} copy-done((bf16[2,512,128]{2,1,0:T(8,128)(2,1)S(1)}, bf16[2,512,128]{2,1,0:T(8,128)(2,1)}, u32[]{:S(2)}) %copy-start.2) | copy-done | bytes 262168
  12.0 0.7 %copy-done.4 = s32[2,4,11]{2,1,0:T(4,128)S(1)} copy-done((s32[2,4,11]{2,1,0:T(4,128)S(1)}, s32[2,4,11]{2,1,0:T(4,128)}, u32[]{:S(2)}) %copy-start.4) | copy-done | bytes 376
  12.7 5.7 %stretch.1 = (f32[4,1024,128]{2,1,0:T(8,128)S(1)}, f32[4,1024,128]{2,1,0:T(8,128)S(1)}, f32[4,1024,128]{2,1,0:T(8,128)S(1)}, f32[8,128]{1,0:T(8,128)S(1)}, s32[14]{0:T(128)S(1)}) custom-call(s32[1]{0:T(128)} %bitcast.own_ref, s32[2,4,11]{2,1,0:T(4,128)S(1)} %copy-done.4, bf16[1024,512]{1,0:T(8,128)(2,1)S(1)} %copy-done, bf16[2,512,128]{2,1,0:T(8,128)(2,1)S(1)} %copy-done.2, ...), custom_call_target="tpu_custom_call" | custom-call | flops 1000 | bytes 1000 | tf_op jit(solution)/shard_map/stretch/pallas_call | solution.py:345
  18.4 0.0 collective-permute-done.1.refs_0_
  18.4 1.3 %collective-permute-done.2.refs_1_ = bf16[2,256,128]{2,1,0:T(8,128)(2,1)S(1)} collective-permute-done((bf16[2,256,128]{2,1,0:T(8,128)(2,1)}, bf16[2,256,128]{2,1,0:T(8,128)(2,1)S(1)}, u32[]{:S(2)}, u32[]{:S(2)}) %collective-permute-start.2) | collective-permute-done | bytes 131104 | tf_op jit(solution)/shard_map/ppermute | solution.py:35
  19.8 0.0 collective-permute-done.3.refs_2_
  19.8 0.3 collective-permute-done.4.refs_3_
  20.1 0.0 collective-permute-done.5.refs_4_
  20.1 0.9 %copy-done.3 = bf16[2,256,128]{2,1,0:T(8,128)(2,1)S(1)} copy-done((bf16[2,256,128]{2,1,0:T(8,128)(2,1)S(1)}, bf16[2,256,128]{2,1,0:T(8,128)(2,1)}, u32[]{:S(2)}) %copy-start.3) | copy-done | bytes 131096
  21.0 0.1 pack.2.refs_0_
  21.1 1.6 %collective-permute-start.6 = (bf16[6,2,256,128]{3,2,1,0:T(8,128)(2,1)S(1)}, bf16[6,2,256,128]{3,2,1,0:T(8,128)(2,1)S(1)}, u32[]{:S(2)}, u32[]{:S(2)}) collective-permute-start(bf16[6,2,256,128]{3,2,1,0:T(8,128)(2,1)S(1)} %pack.2.refs_0_), channel_id=1, source_target_pairs={{0,1},{1,0},{2,3},{3,2},{4,5},{5,4},{6,7},{7,6},{8,9},{9,8},{10,11... | collective-permute-start | bytes 2359304 | tf_op jit(solution)/shard_map/ppermute | solution.py:35
  22.6 0.0 copy-done.6
  22.6 0.0 collective-permute-start.7
  22.6 0.0 copy-done.5
  22.6 4.2 %collective-permute-start.8 = (bf16[2,256,128]{2,1,0:T(8,128)(2,1)S(1)}, bf16[2,256,128]{2,1,0:T(8,128)(2,1)S(1)}, u32[]{:S(2)}, u32[]{:S(2)}) collective-permute-start(bf16[2,256,128]{2,1,0:T(8,128)(2,1)S(1)} %copy-done.5), channel_id=1, source_target_pairs={{0,12},{1,13},{2,14},{3,15},{4,8},{5,9},{6,10},{7,11},{8,4},{9,5},... | collective-permute-start | bytes 393224 | tf_op jit(solution)/shard_map/ppermute | solution.py:35
  26.9 0.0 collective-permute-done.6.refs_1_
  26.9 0.0 copy-done.1
  26.9 12.1 %pages.2 = (f32[4,1024,128]{2,1,0:T(8,128)S(1)}, f32[4,1024,128]{2,1,0:T(8,128)S(1)}, f32[4,1024,128]{2,1,0:T(8,128)S(1)}, f32[8,128]{1,0:T(8,128)S(1)}) custom-call(s32[14]{0:T(128)S(1)} %get-tuple-element.24.list_ref, bf16[1024,512]{1,0:T(8,128)(2,1)S(1)} %copy-done.1, ...), custom_call_target="tpu_custom_call", output_to_operand_aliasing={{0}: (4, {}), {1}: (5, {}), {2}: (6, {})} | custom-call | flops 1000 | bytes 1000 | tf_op jit(solution)/shard_map/pages/pallas_call | solution.py:314
  39.0 0.0 collective-permute-done.7.refs_0_
  39.0 0.0 collective-permute-done.8.refs_1_
  39.0 0.7 %collective-permute-start.9 = (bf16[2,2,256,128]{3,2,1,0:T(8,128)(2,1)S(1)}, bf16[2,2,256,128]{3,2,1,0:T(8,128)(2,1)S(1)}, u32[]{:S(2)}, u32[]{:S(2)}) collective-permute-start(bf16[2,2,256,128]{3,2,1,0:T(8,128)(2,1)S(1)} %pack.3.refs_2_), channel_id=1, source_target_pairs={{0,1},{1,0},{2,3},{3,2},{4,5},{5,4},{6,7},{7,6},{8,9},{9,8},{10,11... | collective-permute-start | bytes 786440 | tf_op jit(solution)/shard_map/ppermute | solution.py:35
  39.7 1.2 %collective-permute-done.9.refs_3_ = bf16[2,2,256,128]{3,2,1,0:T(8,128)(2,1)S(1)} collective-permute-done((bf16[2,2,256,128]{3,2,1,0:T(8,128)(2,1)S(1)}, bf16[2,2,256,128]{3,2,1,0:T(8,128)(2,1)S(1)}, u32[]{:S(2)}, u32[]{:S(2)}) %collective-permute-start.9) | collective-permute-done | bytes 262176 | tf_op jit(solution)/shard_map/ppermute | solution.py:35
  40.9 8.7 %pages.3 = bf16[1024,512]{1,0:T(8,128)(2,1)} custom-call(s32[14]{0:T(128)S(1)} %get-tuple-element.24.list_ref, bf16[1024,512]{1,0:T(8,128)(2,1)S(1)} %copy-done.1, bf16[6,2,256,128]{3,2,1,0:T(8,128)(2,1)S(1)} %pack.2.refs_0_, bf16[6,2,256,128]{3,2,1,0:T(8,128)(2,1)S(1)} %collective-permute-done.6.refs_1_, bf16[2,2,256,128]{3,2,1,0:T(8,128)(2,1)S(1)} %pack.3.refs_2_, ...), custom_call_target="tpu_custom_call" | custom-call | flops 1000 | bytes 1000 | tf_op jit(solution)/shard_map/pages/pallas_call | solution.py:314
  (8 shorter events, 0.0 us)
Async XLA Ops:
  3.1 5.5 %collective-permute-start = (bf16[2,512,128]{2,1,0:T(8,128)(2,1)}, bf16[2,512,128]{2,1,0:T(8,128)(2,1)S(1)}, u32[]{:S(2)}, u32[]{:S(2)}) collective-permute-start(bf16[2,512,128]{2,1,0:T(8,128)(2,1)} %get-tuple-element.23.own_kv_ref), channel_id=1, source_target_pairs={{0,1},{1,0},{2,3},{3,2},{4,5},{5,4},{6,7},{7,6},{8,9},{9,8},{10,11... | collective-permute-start | bytes 786440 | tf_op jit(solution)/shard_map/ppermute | solution.py:35
  3.9 14.6 %collective-permute-start.1 = (bf16[2,256,128]{2,1,0:T(8,128)(2,1)}, bf16[2,256,128]{2,1,0:T(8,128)(2,1)S(1)}, u32[]{:S(2)}, u32[]{:S(2)}) collective-permute-start(bf16[2,256,128]{2,1,0:T(8,128)(2,1)} %get-tuple-element.25), channel_id=1, source_target_pairs={{0,10},{1,11},{2,8},{3,9},{4,14},{5,15},{6,12},{7,13},{8,2},{9,3},... | collective-permute-start | bytes 393224 | tf_op jit(solution)/shard_map/ppermute | solution.py:35
  4.9 14.9 %collective-permute-start.2 = (bf16[2,256,128]{2,1,0:T(8,128)(2,1)}, bf16[2,256,128]{2,1,0:T(8,128)(2,1)S(1)}, u32[]{:S(2)}, u32[]{:S(2)}) collective-permute-start(bf16[2,256,128]{2,1,0:T(8,128)(2,1)} %get-tuple-element.26), channel_id=1, source_target_pairs={{0,8},{1,9},{2,10},{3,11},{4,12},{5,13},{6,14},{7,15},{8,0},{9,1},... | collective-permute-start | bytes 393224 | tf_op jit(solution)/shard_map/ppermute | solution.py:35
  7.2 12.6 %collective-permute-start.3 = (bf16[2,256,128]{2,1,0:T(8,128)(2,1)}, bf16[2,256,128]{2,1,0:T(8,128)(2,1)S(1)}, u32[]{:S(2)}, u32[]{:S(2)}) collective-permute-start(bf16[2,256,128]{2,1,0:T(8,128)(2,1)} %get-tuple-element.27), channel_id=1, source_target_pairs={{0,6},{1,7},{2,4},{3,5},{4,2},{5,3},{6,0},{7,1},{8,14},{9,15},{10,... | collective-permute-start | bytes 393224 | tf_op jit(solution)/shard_map/ppermute | solution.py:35
  7.3 12.8 %collective-permute-start.4 = (bf16[2,256,128]{2,1,0:T(8,128)(2,1)}, bf16[2,256,128]{2,1,0:T(8,128)(2,1)S(1)}, u32[]{:S(2)}, u32[]{:S(2)}) collective-permute-start(bf16[2,256,128]{2,1,0:T(8,128)(2,1)} %get-tuple-element.28), channel_id=1, source_target_pairs={{0,4},{1,5},{2,6},{3,7},{4,0},{5,1},{6,2},{7,3},{8,12},{9,13},{10,... | collective-permute-start | bytes 393224 | tf_op jit(solution)/shard_map/ppermute | solution.py:35
  8.6 11.5 %collective-permute-start.5 = (bf16[2,256,128]{2,1,0:T(8,128)(2,1)}, bf16[2,256,128]{2,1,0:T(8,128)(2,1)S(1)}, u32[]{:S(2)}, u32[]{:S(2)}) collective-permute-start(bf16[2,256,128]{2,1,0:T(8,128)(2,1)} %get-tuple-element.29), channel_id=1, source_target_pairs={{0,2},{1,3},{2,0},{3,1},{4,6},{5,7},{6,4},{7,5},{8,10},{9,11},{10,... | collective-permute-start | bytes 393224 | tf_op jit(solution)/shard_map/ppermute | solution.py:35
  9.9 1.2 %copy-start = (bf16[1024,512]{1,0:T(8,128)(2,1)S(1)}, bf16[1024,512]{1,0:T(8,128)(2,1)}, u32[]{:S(2)}) copy-start(bf16[1024,512]{1,0:T(8,128)(2,1)} %q_ref.5) | copy-start | bytes 3145732
  11.1 0.9 %copy-start.2 = (bf16[2,512,128]{2,1,0:T(8,128)(2,1)S(1)}, bf16[2,512,128]{2,1,0:T(8,128)(2,1)}, u32[]{:S(2)}) copy-start(bf16[2,512,128]{2,1,0:T(8,128)(2,1)} %get-tuple-element.23.own_kv_ref) | copy-start | bytes 786436
  12.0 0.7 %copy-start.4 = (s32[2,4,11]{2,1,0:T(4,128)S(1)}, s32[2,4,11]{2,1,0:T(4,128)}, u32[]{:S(2)}) copy-start(s32[2,4,11]{2,1,0:T(4,128)} %table_ref.3) | copy-start | bytes 1060
  12.7 9.9 %copy-start.6 = (bf16[2,256,128]{2,1,0:T(8,128)(2,1)S(1)}, bf16[2,256,128]{2,1,0:T(8,128)(2,1)}, u32[]{:S(2)}) copy-start(bf16[2,256,128]{2,1,0:T(8,128)(2,1)} %get-tuple-element.32) | copy-start | bytes 393220
  12.7 9.9 %copy-start.5 = (bf16[2,256,128]{2,1,0:T(8,128)(2,1)S(1)}, bf16[2,256,128]{2,1,0:T(8,128)(2,1)}, u32[]{:S(2)}) copy-start(bf16[2,256,128]{2,1,0:T(8,128)(2,1)} %get-tuple-element.33) | copy-start | bytes 393220
  12.7 14.1 %copy-start.1 = (bf16[1024,512]{1,0:T(8,128)(2,1)S(1)}, bf16[1024,512]{1,0:T(8,128)(2,1)}, u32[]{:S(2)}) copy-start(bf16[1024,512]{1,0:T(8,128)(2,1)} %q_ref.5) | copy-start | bytes 3145732
  20.1 0.9 %copy-start.3 = (bf16[2,256,128]{2,1,0:T(8,128)(2,1)S(1)}, bf16[2,256,128]{2,1,0:T(8,128)(2,1)}, u32[]{:S(2)}) copy-start(bf16[2,256,128]{2,1,0:T(8,128)(2,1)} %get-tuple-element.30.refs_5_) | copy-start | bytes 393220
  21.1 5.8 %collective-permute-start.6 = (bf16[6,2,256,128]{3,2,1,0:T(8,128)(2,1)S(1)}, bf16[6,2,256,128]{3,2,1,0:T(8,128)(2,1)S(1)}, u32[]{:S(2)}, u32[]{:S(2)}) collective-permute-start(bf16[6,2,256,128]{3,2,1,0:T(8,128)(2,1)S(1)} %pack.2.refs_0_), channel_id=1, source_target_pairs={{0,1},{1,0},{2,3},{3,2},{4,5},{5,4},{6,7},{7,6},{8,9},{9,8},{10,11... | collective-permute-start | bytes 2359304 | tf_op jit(solution)/shard_map/ppermute | solution.py:35
  22.6 16.4 %collective-permute-start.7 = (bf16[2,256,128]{2,1,0:T(8,128)(2,1)S(1)}, bf16[2,256,128]{2,1,0:T(8,128)(2,1)S(1)}, u32[]{:S(2)}, u32[]{:S(2)}) collective-permute-start(bf16[2,256,128]{2,1,0:T(8,128)(2,1)S(1)} %copy-done.6), channel_id=1, source_target_pairs={{0,14},{1,15},{2,12},{3,13},{4,10},{5,11},{6,8},{7,9},{8,6},{9,7},... | collective-permute-start | bytes 393224 | tf_op jit(solution)/shard_map/ppermute | solution.py:35
  22.6 16.4 %collective-permute-start.8 = (bf16[2,256,128]{2,1,0:T(8,128)(2,1)S(1)}, bf16[2,256,128]{2,1,0:T(8,128)(2,1)S(1)}, u32[]{:S(2)}, u32[]{:S(2)}) collective-permute-start(bf16[2,256,128]{2,1,0:T(8,128)(2,1)S(1)} %copy-done.5), channel_id=1, source_target_pairs={{0,12},{1,13},{2,14},{3,15},{4,8},{5,9},{6,10},{7,11},{8,4},{9,5},... | collective-permute-start | bytes 393224 | tf_op jit(solution)/shard_map/ppermute | solution.py:35
  39.0 1.9 %collective-permute-start.9 = (bf16[2,2,256,128]{3,2,1,0:T(8,128)(2,1)S(1)}, bf16[2,2,256,128]{3,2,1,0:T(8,128)(2,1)S(1)}, u32[]{:S(2)}, u32[]{:S(2)}) collective-permute-start(bf16[2,2,256,128]{3,2,1,0:T(8,128)(2,1)S(1)} %pack.3.refs_2_), channel_id=1, source_target_pairs={{0,1},{1,0},{2,3},{3,2},{4,5},{5,4},{6,7},{7,6},{8,9},{9,8},{10,11... | collective-permute-start | bytes 786440 | tf_op jit(solution)/shard_map/ppermute | solution.py:35
where the time goes:
time: 50.5 us; the launch traced here: 49.7 us
  Pallas kernels  29.6 us (59%)
  starting transfers between devices  13.2 us (26%)
  local copies, waits for them, and re-layouts  3.78 us (7%)
  waiting for transfers between devices  2.84 us (6%)
    pallas_call x2, Pallas kernels, attend_pages(): pl.pallas_call(functools.partial(pages_kernel, final), out_shape=jax.Shap...  20.8 us
    ppermute x10, starting transfers between devices, swapped(): return lax.ppermute(value, axis, pairs)  13.2 us
    pallas_call x1, Pallas kernels, shards(): pl.pallas_call(functools.partial(stretch_kernel, cuts), out_shape=[s_shap...  5.7 us
    unnamed x14, local copies, waits for them, and re-layouts  3.78 us
    pallas_call x1, Pallas kernels, pick(): pl.pallas_call(functools.partial(pick_kernel, offsets), out_shape=[jax.Sh...  3.12 us
    ppermute x10, waiting for transfers between devices, swapped(): return lax.ppermute(value, axis, pairs)  2.84 us
  transfers between devices with their start and end apart: 10, of which 3 were waited for; matrix products, arithmetic and copies ran while one was open for 0% of the time, Pallas kernels for 36%

commit v1 on v0

--- a/solution.py
+++ b/solution.py
@@ -145,13 +145,11 @@
             offset = jnp.bitwise_xor(device // CORES, chip)
             inside = (slot >= 0) & (offset >= cuts[wave]) & (offset < cuts[wave + 1])
 
-            @pl.when(inside)
-            def _():
-                list_ref[HEAD + seen] = (cuts[wave + 1] - 1 - offset) * 2 + jnp.bitwise_xor(device % CORES, core)
-
+            place = (cuts[wave + 1] - 1 - offset) * 2 + jnp.bitwise_xor(device % CORES, core)
+            list_ref[HEAD + jnp.where(inside, seen, depth)] = place
             return seen + inside.astype(jnp.int32)
 
-        seen = lax.fori_loop(0, depth, look, seen)
+        seen = lax.fori_loop(0, depth, look, seen, unroll=True)
         list_ref[wave] = seen
     early = list_ref[WAVES - 2]
     late = seen - early
@@ -160,7 +158,9 @@
     list_ref[WAVES] = jnp.where(more, early, early - rest)
 
 
-def stretch_kernel(cuts, own_ref, table_ref, q_ref, own_kv_ref, other_kv_ref, m_ref, l_ref, a_ref, done_ref, list_ref, ks, vs):
+def stretch_kernel(cuts, own_ref, table_ref, q_ref, own_kv_ref, other_kv_ref, page_ref, *refs):
+    m_ref, l_ref, a_ref, done_ref, page_out_ref, list_ref, ks, vs = refs
+    page_out_ref[...] = page_ref[...]
     list_pages(cuts, own_ref[0], table_ref, list_ref)
     half = own_ref[0] % CORES
     rows = own_kv_ref.shape[1]
@@ -306,7 +306,7 @@
     most = CORES * cuts[WAVES - 1]
     if final:
         most = BLOCK - 1 + CORES * (cuts[WAVES] - cuts[WAVES - 1])
-    most = min(pages.shape[0] - HEAD, most)
+    most = min(pages.shape[0] - HEAD - 1, most)
     most = -(-most // BLOCK) * BLOCK
     s_shape = jax.ShapeDtypeStruct(state[0].shape, jnp.float32)
     at = 2 + 2 * waves
@@ -342,11 +342,16 @@
 
     other_stretch = swapped(stretch, "pool", 1)
     s_shape = jax.ShapeDtypeStruct((heads, STRETCH, HD), jnp.float32)
-    *state, pages = pl.pallas_call(
+    *state, got[0], pages = pl.pallas_call(
         functools.partial(stretch_kernel, cuts),
-        out_shape=[s_shape] * 3 + [DONE, jax.ShapeDtypeStruct((HEAD + page_table.shape[2],), jnp.int32)],
-        in_specs=[SMEM, SMEM] + [VMEM] * 3,
-        out_specs=[VMEM] * 4 + [SMEM],
+        out_shape=[s_shape] * 3
+        + [
+            DONE,
+            jax.ShapeDtypeStruct(got[0].shape, got[0].dtype),
+            jax.ShapeDtypeStruct((HEAD + page_table.shape[2] + 1,), jnp.int32),
+        ],
+        in_specs=[SMEM, SMEM] + [VMEM] * 4,
+        out_specs=[VMEM] * 5 + [SMEM],
         scratch_shapes=[
             pltpu.VMEM((STRETCH, HD), jnp.bfloat16),
             pltpu.VMEM((STRETCH, HD), jnp.bfloat16),
@@ -354,7 +359,7 @@
         compiler_params=pltpu.CompilerParams(vmem_limit_bytes=VMEM_BYTES),
         cost_estimate=COST,
         name="stretch",
-    )(own, page_table, queries, stretch, other_stretch)
+    )(own, page_table, queries, stretch, other_stretch, got[0])
 
     received = []
     after = state[3:]

time: 50.5 us -> 49.6 us (0.982)
  the two profiles are of different devices: /device:TPU:27 before, /device:TPU:3 now
where the time goes in v1:
time: 49.6 us; the launch traced here: 48.6 us
  Pallas kernels  29.3 us (59%)
  starting transfers between devices  13.6 us (27%)
  local copies, waits for them, and re-layouts  3.77 us (8%)
  waiting for transfers between devices  1.71 us (3%)
    pallas_call x2, Pallas kernels, attend_pages(): pl.pallas_call(functools.partial(pages_kernel, final), out_shape=jax.Shap...  20.8 us
    ppermute x10, starting transfers between devices, swapped(): return lax.ppermute(value, axis, pairs)  13.6 us
    pallas_call x1, Pallas kernels, shards(): pl.pallas_call(functools.partial(stretch_kernel, cuts), out_shape=[s_shap...  5.34 us
    unnamed x14, local copies, waits for them, and re-layouts  3.77 us
    pallas_call x1, Pallas kernels, pick(): pl.pallas_call(functools.partial(pick_kernel, offsets), out_shape=[jax.Sh...  3.12 us
    ppermute x10, waiting for transfers between devices, swapped(): return lax.ppermute(value, axis, pairs)  1.71 us
  transfers between devices with their start and end apart: 10, of which 2 were waited for; matrix products, arithmetic and copies ran while one was open for 0% of the time, Pallas kernels for 36%

profile of v1, /device:TPU:3, one launch (start us, length us, event | category | flops | bytes accessed | tf_op | source)
XLA Modules:
  0.0 48.6 jit_solution(12251350513866503499)
XLA Ops:
  0.0 3.1 %pick.1 = (bf16[2,256,128]{2,1,0:T(8,128)(2,1)}, bf16[2,256,128]{2,1,0:T(8,128)(2,1)}, bf16[2,256,128]{2,1,0:T(8,128)(2,1)}, bf16[2,256,128]{2,1,0:T(8,128)(2,1)...) custom-call(s32[1]{0:T(128)} %bitcast.own_ref, ...), custom_call_target="tpu_custom_call" | custom-call | tf_op jit(solution)/shard_map/pick/pallas_call | solution.py:77
  3.1 0.7 %collective-permute-start = (bf16[2,512,128]{2,1,0:T(8,128)(2,1)}, bf16[2,512,128]{2,1,0:T(8,128)(2,1)S(1)}, u32[]{:S(2)}, u32[]{:S(2)}) collective-permute-start(bf16[2,512,128]{2,1,0:T(8,128)(2,1)} %get-tuple-element.24.own_kv_ref), channel_id=1, source_target_pairs={{0,1},{1,0},{2,3},{3,2},{4,5},{5,4},{6,7},{7,6},{8,9},{9,8},{10,11... | collective-permute-start | bytes 786440 | tf_op jit(solution)/shard_map/ppermute | solution.py:35
  3.9 3.3 %collective-permute-start.1 = (bf16[2,256,128]{2,1,0:T(8,128)(2,1)}, bf16[2,256,128]{2,1,0:T(8,128)(2,1)S(1)}, u32[]{:S(2)}, u32[]{:S(2)}) collective-permute-start(bf16[2,256,128]{2,1,0:T(8,128)(2,1)} %get-tuple-element.27), channel_id=1, source_target_pairs={{0,10},{1,11},{2,8},{3,9},{4,14},{5,15},{6,12},{7,13},{8,2},{9,3},... | collective-permute-start | bytes 393224 | tf_op jit(solution)/shard_map/ppermute | solution.py:35
  7.1 0.1 collective-permute-start.2
  7.2 1.2 %collective-permute-start.3 = (bf16[2,256,128]{2,1,0:T(8,128)(2,1)}, bf16[2,256,128]{2,1,0:T(8,128)(2,1)S(1)}, u32[]{:S(2)}, u32[]{:S(2)}) collective-permute-start(bf16[2,256,128]{2,1,0:T(8,128)(2,1)} %get-tuple-element.29), channel_id=1, source_target_pairs={{0,6},{1,7},{2,4},{3,5},{4,2},{5,3},{6,0},{7,1},{8,14},{9,15},{10,... | collective-permute-start | bytes 393224 | tf_op jit(solution)/shard_map/ppermute | solution.py:35
  8.4 0.2 collective-permute-start.4
  8.6 0.0 collective-permute-done.other_kv_ref
  8.6 1.2 %collective-permute-start.5 = (bf16[2,256,128]{2,1,0:T(8,128)(2,1)}, bf16[2,256,128]{2,1,0:T(8,128)(2,1)S(1)}, u32[]{:S(2)}, u32[]{:S(2)}) collective-permute-start(bf16[2,256,128]{2,1,0:T(8,128)(2,1)} %get-tuple-element.31), channel_id=1, source_target_pairs={{0,2},{1,3},{2,0},{3,1},{4,6},{5,7},{6,4},{7,5},{8,10},{9,11},{10,... | collective-permute-start | bytes 393224 | tf_op jit(solution)/shard_map/ppermute | solution.py:35
  9.9 1.2 %copy-done = bf16[1024,512]{1,0:T(8,128)(2,1)S(1)} copy-done((bf16[1024,512]{1,0:T(8,128)(2,1)S(1)}, bf16[1024,512]{1,0:T(8,128)(2,1)}, u32[]{:S(2)}) %copy-start) | copy-done | bytes 1048600
  11.1 0.9 %copy-done.2 = bf16[2,512,128]{2,1,0:T(8,128)(2,1)S(1)} copy-done((bf16[2,512,128]{2,1,0:T(8,128)(2,1)S(1)}, bf16[2,512,128]{2,1,0:T(8,128)(2,1)}, u32[]{:S(2)}) %copy-start.2) | copy-done | bytes 262168
  12.0 0.9 %copy-done.3 = bf16[2,256,128]{2,1,0:T(8,128)(2,1)S(1)} copy-done((bf16[2,256,128]{2,1,0:T(8,128)(2,1)S(1)}, bf16[2,256,128]{2,1,0:T(8,128)(2,1)}, u32[]{:S(2)}) %copy-start.3) | copy-done | bytes 131096
  12.9 0.7 %copy-done.4 = s32[2,4,11]{2,1,0:T(4,128)S(1)} copy-done((s32[2,4,11]{2,1,0:T(4,128)S(1)}, s32[2,4,11]{2,1,0:T(4,128)}, u32[]{:S(2)}) %copy-start.4) | copy-done | bytes 376
  13.6 5.3 %stretch.1 = (f32[4,1024,128]{2,1,0:T(8,128)S(1)}, f32[4,1024,128]{2,1,0:T(8,128)S(1)}, f32[4,1024,128]{2,1,0:T(8,128)S(1)}, f32[8,128]{1,0:T(8,128)S(1)}, bf16[...) custom-call(s32[1]{0:T(128)} %bitcast.own_ref, s32[2,4,11]{2,1,0:T(4,128)S(1)} %copy-done.4, bf16[1024,512]{1,0:T(8,128)(2,1)S(1)} %copy-done, ...), custom_call_target="tpu_custom_call" | custom-call | flops 1000 | bytes 1000 | tf_op jit(solution)/shard_map/stretch/pallas_call | solution.py:345
  19.0 0.0 collective-permute-done.1.refs_0_
  19.0 0.5 %collective-permute-done.2.refs_1_ = bf16[2,256,128]{2,1,0:T(8,128)(2,1)S(1)} collective-permute-done((bf16[2,256,128]{2,1,0:T(8,128)(2,1)}, bf16[2,256,128]{2,1,0:T(8,128)(2,1)S(1)}, u32[]{:S(2)}, u32[]{:S(2)}) %collective-permute-start.2) | collective-permute-done | bytes 131104 | tf_op jit(solution)/shard_map/ppermute | solution.py:35
  19.5 0.0 collective-permute-done.3.refs_2_
  19.5 0.0 collective-permute-done.4.refs_3_
  19.5 0.0 collective-permute-done.5.refs_4_
  19.5 0.1 pack.2.refs_0_
  19.6 1.2 %collective-permute-start.6 = (bf16[6,2,256,128]{3,2,1,0:T(8,128)(2,1)S(1)}, bf16[6,2,256,128]{3,2,1,0:T(8,128)(2,1)S(1)}, u32[]{:S(2)}, u32[]{:S(2)}) collective-permute-start(bf16[6,2,256,128]{3,2,1,0:T(8,128)(2,1)S(1)} %pack.2.refs_0_), channel_id=1, source_target_pairs={{0,1},{1,0},{2,3},{3,2},{4,5},{5,4},{6,7},{7,6},{8,9},{9,8},{10,11... | collective-permute-start | bytes 2359304 | tf_op jit(solution)/shard_map/ppermute | solution.py:35
  20.7 0.0 copy-done.6
  20.7 5.3 %collective-permute-start.7 = (bf16[2,256,128]{2,1,0:T(8,128)(2,1)S(1)}, bf16[2,256,128]{2,1,0:T(8,128)(2,1)S(1)}, u32[]{:S(2)}, u32[]{:S(2)}) collective-permute-start(bf16[2,256,128]{2,1,0:T(8,128)(2,1)S(1)} %copy-done.6), channel_id=1, source_target_pairs={{0,14},{1,15},{2,12},{3,13},{4,10},{5,11},{6,8},{7,9},{8,6},{9,7},... | collective-permute-start | bytes 393224 | tf_op jit(solution)/shard_map/ppermute | solution.py:35
  26.0 0.0 copy-done.5
  26.0 0.0 collective-permute-start.8
  26.0 0.0 collective-permute-done.6.refs_1_
  26.0 0.0 copy-done.1
  26.0 12.1 %pages.2 = (f32[4,1024,128]{2,1,0:T(8,128)S(1)}, f32[4,1024,128]{2,1,0:T(8,128)S(1)}, f32[4,1024,128]{2,1,0:T(8,128)S(1)}, f32[8,128]{1,0:T(8,128)S(1)}) custom-call(s32[15]{0:T(128)S(1)} %get-tuple-element.26.list_ref, bf16[1024,512]{1,0:T(8,128)(2,1)S(1)} %copy-done.1, ...), custom_call_target="tpu_custom_call", output_to_operand_aliasing={{0}: (4, {}), {1}: (5, {}), {2}: (6, {})} | custom-call | flops 1000 | bytes 1000 | tf_op jit(solution)/shard_map/pages/pallas_call | solution.py:314
  38.2 0.0 collective-permute-done.7.refs_0_
  38.2 0.0 collective-permute-done.8.refs_1_
  38.2 0.4 collective-permute-start.9
  38.6 1.2 %collective-permute-done.9.refs_3_ = bf16[2,2,256,128]{3,2,1,0:T(8,128)(2,1)S(1)} collective-permute-done((bf16[2,2,256,128]{3,2,1,0:T(8,128)(2,1)S(1)}, bf16[2,2,256,128]{3,2,1,0:T(8,128)(2,1)S(1)}, u32[]{:S(2)}, u32[]{:S(2)}) %collective-permute-start.9) | collective-permute-done | bytes 262176 | tf_op jit(solution)/shard_map/ppermute | solution.py:35
  39.8 8.6 %pages.3 = bf16[1024,512]{1,0:T(8,128)(2,1)} custom-call(s32[15]{0:T(128)S(1)} %get-tuple-element.26.list_ref, bf16[1024,512]{1,0:T(8,128)(2,1)S(1)} %copy-done.1, bf16[6,2,256,128]{3,2,1,0:T(8,128)(2,1)S(1)} %pack.2.refs_0_, bf16[6,2,256,128]{3,2,1,0:T(8,128)(2,1)S(1)} %collective-permute-done.6.refs_1_, bf16[2,2,256,128]{3,2,1,0:T(8,128)(2,1)S(1)} %pack.3.refs_2_, ...), custom_call_target="tpu_custom_call" | custom-call | flops 1000 | bytes 1000 | tf_op jit(solution)/shard_map/pages/pallas_call | solution.py:314
  (8 shorter events, 0.0 us)
Async XLA Ops:
  3.1 5.5 %collective-permute-start = (bf16[2,512,128]{2,1,0:T(8,128)(2,1)}, bf16[2,512,128]{2,1,0:T(8,128)(2,1)S(1)}, u32[]{:S(2)}, u32[]{:S(2)}) collective-permute-start(bf16[2,512,128]{2,1,0:T(8,128)(2,1)} %get-tuple-element.24.own_kv_ref), channel_id=1, source_target_pairs={{0,1},{1,0},{2,3},{3,2},{4,5},{5,4},{6,7},{7,6},{8,9},{9,8},{10,11... | collective-permute-start | bytes 786440 | tf_op jit(solution)/shard_map/ppermute | solution.py:35
  3.9 15.1 %collective-permute-start.1 = (bf16[2,256,128]{2,1,0:T(8,128)(2,1)}, bf16[2,256,128]{2,1,0:T(8,128)(2,1)S(1)}, u32[]{:S(2)}, u32[]{:S(2)}) collective-permute-start(bf16[2,256,128]{2,1,0:T(8,128)(2,1)} %get-tuple-element.27), channel_id=1, source_target_pairs={{0,10},{1,11},{2,8},{3,9},{4,14},{5,15},{6,12},{7,13},{8,2},{9,3},... | collective-permute-start | bytes 393224 | tf_op jit(solution)/shard_map/ppermute | solution.py:35
  7.1 12.3 %collective-permute-start.2 = (bf16[2,256,128]{2,1,0:T(8,128)(2,1)}, bf16[2,256,128]{2,1,0:T(8,128)(2,1)S(1)}, u32[]{:S(2)}, u32[]{:S(2)}) collective-permute-start(bf16[2,256,128]{2,1,0:T(8,128)(2,1)} %get-tuple-element.28), channel_id=1, source_target_pairs={{0,8},{1,9},{2,10},{3,11},{4,12},{5,13},{6,14},{7,15},{8,0},{9,1},... | collective-permute-start | bytes 393224 | tf_op jit(solution)/shard_map/ppermute | solution.py:35
  7.2 12.3 %collective-permute-start.3 = (bf16[2,256,128]{2,1,0:T(8,128)(2,1)}, bf16[2,256,128]{2,1,0:T(8,128)(2,1)S(1)}, u32[]{:S(2)}, u32[]{:S(2)}) collective-permute-start(bf16[2,256,128]{2,1,0:T(8,128)(2,1)} %get-tuple-element.29), channel_id=1, source_target_pairs={{0,6},{1,7},{2,4},{3,5},{4,2},{5,3},{6,0},{7,1},{8,14},{9,15},{10,... | collective-permute-start | bytes 393224 | tf_op jit(solution)/shard_map/ppermute | solution.py:35
  8.4 11.0 %collective-permute-start.4 = (bf16[2,256,128]{2,1,0:T(8,128)(2,1)}, bf16[2,256,128]{2,1,0:T(8,128)(2,1)S(1)}, u32[]{:S(2)}, u32[]{:S(2)}) collective-permute-start(bf16[2,256,128]{2,1,0:T(8,128)(2,1)} %get-tuple-element.30), channel_id=1, source_target_pairs={{0,4},{1,5},{2,6},{3,7},{4,0},{5,1},{6,2},{7,3},{8,12},{9,13},{10,... | collective-permute-start | bytes 393224 | tf_op jit(solution)/shard_map/ppermute | solution.py:35
  8.6 10.9 %collective-permute-start.5 = (bf16[2,256,128]{2,1,0:T(8,128)(2,1)}, bf16[2,256,128]{2,1,0:T(8,128)(2,1)S(1)}, u32[]{:S(2)}, u32[]{:S(2)}) collective-permute-start(bf16[2,256,128]{2,1,0:T(8,128)(2,1)} %get-tuple-element.31), channel_id=1, source_target_pairs={{0,2},{1,3},{2,0},{3,1},{4,6},{5,7},{6,4},{7,5},{8,10},{9,11},{10,... | collective-permute-start | bytes 393224 | tf_op jit(solution)/shard_map/ppermute | solution.py:35
  9.9 1.2 %copy-start = (bf16[1024,512]{1,0:T(8,128)(2,1)S(1)}, bf16[1024,512]{1,0:T(8,128)(2,1)}, u32[]{:S(2)}) copy-start(bf16[1024,512]{1,0:T(8,128)(2,1)} %q_ref.5) | copy-start | bytes 3145732
  11.1 0.9 %copy-start.2 = (bf16[2,512,128]{2,1,0:T(8,128)(2,1)S(1)}, bf16[2,512,128]{2,1,0:T(8,128)(2,1)}, u32[]{:S(2)}) copy-start(bf16[2,512,128]{2,1,0:T(8,128)(2,1)} %get-tuple-element.24.own_kv_ref) | copy-start | bytes 786436
  12.0 0.9 %copy-start.3 = (bf16[2,256,128]{2,1,0:T(8,128)(2,1)S(1)}, bf16[2,256,128]{2,1,0:T(8,128)(2,1)}, u32[]{:S(2)}) copy-start(bf16[2,256,128]{2,1,0:T(8,128)(2,1)} %get-tuple-element.25.page_ref) | copy-start | bytes 393220
  12.9 0.7 %copy-start.4 = (s32[2,4,11]{2,1,0:T(4,128)S(1)}, s32[2,4,11]{2,1,0:T(4,128)}, u32[]{:S(2)}) copy-start(s32[2,4,11]{2,1,0:T(4,128)} %table_ref.3) | copy-start | bytes 1060
  13.6 7.1 %copy-start.6 = (bf16[2,256,128]{2,1,0:T(8,128)(2,1)S(1)}, bf16[2,256,128]{2,1,0:T(8,128)(2,1)}, u32[]{:S(2)}) copy-start(bf16[2,256,128]{2,1,0:T(8,128)(2,1)} %get-tuple-element.34) | copy-start | bytes 393220
  13.6 12.4 %copy-start.5 = (bf16[2,256,128]{2,1,0:T(8,128)(2,1)S(1)}, bf16[2,256,128]{2,1,0:T(8,128)(2,1)}, u32[]{:S(2)}) copy-start(bf16[2,256,128]{2,1,0:T(8,128)(2,1)} %get-tuple-element.35) | copy-start | bytes 393220
  13.6 12.4 %copy-start.1 = (bf16[1024,512]{1,0:T(8,128)(2,1)S(1)}, bf16[1024,512]{1,0:T(8,128)(2,1)}, u32[]{:S(2)}) copy-start(bf16[1024,512]{1,0:T(8,128)(2,1)} %q_ref.5) | copy-start | bytes 3145732
  19.6 6.5 %collective-permute-start.6 = (bf16[6,2,256,128]{3,2,1,0:T(8,128)(2,1)S(1)}, bf16[6,2,256,128]{3,2,1,0:T(8,128)(2,1)S(1)}, u32[]{:S(2)}, u32[]{:S(2)}) collective-permute-start(bf16[6,2,256,128]{3,2,1,0:T(8,128)(2,1)S(1)} %pack.2.refs_0_), channel_id=1, source_target_pairs={{0,1},{1,0},{2,3},{3,2},{4,5},{5,4},{6,7},{7,6},{8,9},{9,8},{10,11... | collective-permute-start | bytes 2359304 | tf_op jit(solution)/shard_map/ppermute | solution.py:35
  20.7 17.5 %collective-permute-start.7 = (bf16[2,256,128]{2,1,0:T(8,128)(2,1)S(1)}, bf16[2,256,128]{2,1,0:T(8,128)(2,1)S(1)}, u32[]{:S(2)}, u32[]{:S(2)}) collective-permute-start(bf16[2,256,128]{2,1,0:T(8,128)(2,1)S(1)} %copy-done.6), channel_id=1, source_target_pairs={{0,14},{1,15},{2,12},{3,13},{4,10},{5,11},{6,8},{7,9},{8,6},{9,7},... | collective-permute-start | bytes 393224 | tf_op jit(solution)/shard_map/ppermute | solution.py:35
  26.0 12.2 %collective-permute-start.8 = (bf16[2,256,128]{2,1,0:T(8,128)(2,1)S(1)}, bf16[2,256,128]{2,1,0:T(8,128)(2,1)S(1)}, u32[]{:S(2)}, u32[]{:S(2)}) collective-permute-start(bf16[2,256,128]{2,1,0:T(8,128)(2,1)S(1)} %copy-done.5), channel_id=1, source_target_pairs={{0,12},{1,13},{2,14},{3,15},{4,8},{5,9},{6,10},{7,11},{8,4},{9,5},... | collective-permute-start | bytes 393224 | tf_op jit(solution)/shard_map/ppermute | solution.py:35
  38.2 1.6 %collective-permute-start.9 = (bf16[2,2,256,128]{3,2,1,0:T(8,128)(2,1)S(1)}, bf16[2,2,256,128]{3,2,1,0:T(8,128)(2,1)S(1)}, u32[]{:S(2)}, u32[]{:S(2)}) collective-permute-start(bf16[2,2,256,128]{3,2,1,0:T(8,128)(2,1)S(1)} %pack.3.refs_2_), channel_id=1, source_target_pairs={{0,1},{1,0},{2,3},{3,2},{4,5},{5,4},{6,7},{7,6},{8,9},{9,8},{10,11... | collective-permute-start | bytes 786440 | tf_op jit(solution)/shard_map/ppermute | solution.py:35

commit v2 on v1

--- a/solution.py
+++ b/solution.py
@@ -61,12 +61,18 @@
         slots.append(lax.fori_loop(0, depth, look, 0, unroll=True))
     for copy in loads:
         copy.wait()
+    rows = new_keys_ref.shape[0]
+    targets = [[out.at[side] for side in range(2)] for out in outs]
+    targets.append([new_out.at[side, pl.ds(rows, PAGE)] for side in range(2)])
     stores = [
-        pltpu.make_async_copy(held.at[side, slot], out.at[side], sent.at[at, side])
-        for at, (out, slot) in enumerate(zip(outs, slots))
+        pltpu.make_async_copy(held.at[side, slot], target[side], sent.at[at, side])
+        for at, (target, slot) in enumerate(zip(targets, slots))
         for side in range(2)
     ]
-    stores.append(pltpu.make_async_copy(new_held, new_out, sent.at[len(offsets), 0]))
+    stores += [
+        pltpu.make_async_copy(new_held.at[side], new_out.at[side, pl.ds(0, rows)], sent.at[len(offsets), side])
+        for side in range(2)
+    ]
     for copy in stores:
         copy.start()
     for copy in stores:
@@ -76,10 +82,10 @@
 def pick(own, table, keys, values, new_keys, new_values, offsets):
     return pl.pallas_call(
         functools.partial(pick_kernel, offsets),
-        out_shape=[jax.ShapeDtypeStruct((2, PAGE, HD), keys.dtype)] * len(offsets)
-        + [jax.ShapeDtypeStruct((2,) + new_keys.shape, new_keys.dtype)],
+        out_shape=[jax.ShapeDtypeStruct((2, PAGE, HD), keys.dtype)] * (len(offsets) - 1)
+        + [jax.ShapeDtypeStruct((2, new_keys.shape[0] + PAGE, HD), new_keys.dtype)],
         in_specs=[SMEM, SMEM] + [ANY] * 4,
-        out_specs=[ANY] * (len(offsets) + 1),
+        out_specs=[ANY] * len(offsets),
         scratch_shapes=[
             pltpu.VMEM((2,) + keys.shape, keys.dtype),
             pltpu.VMEM((2,) + new_keys.shape, new_keys.dtype),
@@ -158,15 +164,15 @@
     list_ref[WAVES] = jnp.where(more, early, early - rest)
 
 
-def stretch_kernel(cuts, own_ref, table_ref, q_ref, own_kv_ref, other_kv_ref, page_ref, *refs):
+def stretch_kernel(cuts, own_ref, table_ref, q_ref, own_kv_ref, other_kv_ref, *refs):
     m_ref, l_ref, a_ref, done_ref, page_out_ref, list_ref, ks, vs = refs
-    page_out_ref[...] = page_ref[...]
     list_pages(cuts, own_ref[0], table_ref, list_ref)
     half = own_ref[0] % CORES
-    rows = own_kv_ref.shape[1]
+    rows = own_kv_ref.shape[1] - PAGE
+    page_out_ref[...] = own_kv_ref[:, rows:]
     for place, source in ((half, own_kv_ref), (1 - half, other_kv_ref)):
         for side, target in enumerate((ks, vs)):
-            target[pl.ds(pl.multiple_of(place * rows, rows), rows)] = source[side]
+            target[pl.ds(pl.multiple_of(place * rows, rows), rows)] = source[side, :rows]
     done_ref[...] = jnp.zeros_like(done_ref)
 
     tiles = STRETCH // TILE
@@ -337,8 +343,8 @@
     cuts = (0, chips * 3 // 4, chips)
     order = list(range(chips // 2, chips)) + list(range(1, chips // 2)) + [0]
     *pages, stretch = pick(own, page_table, pool_keys, pool_values, stretch_keys, stretch_values, order)
-    picked = dict(zip(order, pages))
-    got = {at: picked[at] if at == 0 else swapped(picked[at], "pool", at * CORES) for at in order}
+    picked = dict(zip(order[:-1], pages))
+    got = {at: swapped(picked[at], "pool", at * CORES) for at in order[:-1]}
 
     other_stretch = swapped(stretch, "pool", 1)
     s_shape = jax.ShapeDtypeStruct((heads, STRETCH, HD), jnp.float32)
@@ -347,10 +353,10 @@
         out_shape=[s_shape] * 3
         + [
             DONE,
-            jax.ShapeDtypeStruct(got[0].shape, got[0].dtype),
+            jax.ShapeDtypeStruct((2, PAGE, HD), stretch.dtype),
             jax.ShapeDtypeStruct((HEAD + page_table.shape[2] + 1,), jnp.int32),
         ],
-        in_specs=[SMEM, SMEM] + [VMEM] * 4,
+        in_specs=[SMEM, SMEM] + [VMEM] * 3,
         out_specs=[VMEM] * 5 + [SMEM],
         scratch_shapes=[
             pltpu.VMEM((STRETCH, HD), jnp.bfloat16),
@@ -359,7 +365,7 @@
         compiler_params=pltpu.CompilerParams(vmem_limit_bytes=VMEM_BYTES),
         cost_estimate=COST,
         name="stretch",
-    )(own, page_table, queries, stretch, other_stretch, got[0])
+    )(own, page_table, queries, stretch, other_stretch)
 
     received = []
     after = state[3:]

time: 49.6 us -> 49.1 us (0.990)
  the two profiles are of different devices: /device:TPU:3 before, /device:TPU:25 now
where the time goes in v2:
time: 49.1 us; the launch traced here: 48.8 us
  Pallas kernels  29.3 us (60%)
  starting transfers between devices  13.2 us (27%)
  waiting for transfers between devices  3.16 us (6%)
  local copies, waits for them, and re-layouts  2.92 us (6%)
    pallas_call x2, Pallas kernels, attend_pages(): pl.pallas_call(functools.partial(pages_kernel, final), out_shape=jax.Shap...  20.8 us
    ppermute x10, starting transfers between devices, swapped(): return lax.ppermute(value, axis, pairs)  13.2 us
    pallas_call x1, Pallas kernels, shards(): pl.pallas_call(functools.partial(stretch_kernel, cuts), out_shape=[s_shap...  5.33 us
    ppermute x10, waiting for transfers between devices, swapped(): return lax.ppermute(value, axis, pairs)  3.16 us
    pallas_call x1, Pallas kernels, pick(): pl.pallas_call(functools.partial(pick_kernel, offsets), out_shape=[jax.Sh...  3.11 us
    unnamed x12, local copies, waits for them, and re-layouts  2.92 us
  transfers between devices with their start and end apart: 10, of which 3 were waited for; matrix products, arithmetic and copies ran while one was open for 0% of the time, Pallas kernels for 36%

profile of v2, /device:TPU:25, one launch (start us, length us, event | category | flops | bytes accessed | tf_op | source)
XLA Modules:
  0.0 48.8 jit_solution(14815278757878905558)
XLA Ops:
  0.0 3.1 %pick.1 = (bf16[2,256,128]{2,1,0:T(8,128)(2,1)}, bf16[2,256,128]{2,1,0:T(8,128)(2,1)}, bf16[2,256,128]{2,1,0:T(8,128)(2,1)}, bf16[2,256,128]{2,1,0:T(8,128)(2,1)...) custom-call(s32[1]{0:T(128)} %bitcast.own_ref, ...), custom_call_target="tpu_custom_call" | custom-call | tf_op jit(solution)/shard_map/pick/pallas_call | solution.py:83
  3.1 0.7 %collective-permute-start = (bf16[2,768,128]{2,1,0:T(8,128)(2,1)}, bf16[2,768,128]{2,1,0:T(8,128)(2,1)S(1)}, u32[]{:S(2)}, u32[]{:S(2)}) collective-permute-start(bf16[2,768,128]{2,1,0:T(8,128)(2,1)} %get-tuple-element.23.own_kv_ref), channel_id=1, source_target_pairs={{0,1},{1,0},{2,3},{3,2},{4,5},{5,4},{6,7},{7,6},{8,9},{9,8},{10,11... | collective-permute-start | bytes 1179656 | tf_op jit(solution)/shard_map/ppermute | solution.py:35
  3.9 1.0 %collective-permute-start.1 = (bf16[2,256,128]{2,1,0:T(8,128)(2,1)}, bf16[2,256,128]{2,1,0:T(8,128)(2,1)S(1)}, u32[]{:S(2)}, u32[]{:S(2)}) collective-permute-start(bf16[2,256,128]{2,1,0:T(8,128)(2,1)} %get-tuple-element.25), channel_id=1, source_target_pairs={{0,10},{1,11},{2,8},{3,9},{4,14},{5,15},{6,12},{7,13},{8,2},{9,3},... | collective-permute-start | bytes 393224 | tf_op jit(solution)/shard_map/ppermute | solution.py:35
  4.9 2.3 %collective-permute-start.2 = (bf16[2,256,128]{2,1,0:T(8,128)(2,1)}, bf16[2,256,128]{2,1,0:T(8,128)(2,1)S(1)}, u32[]{:S(2)}, u32[]{:S(2)}) collective-permute-start(bf16[2,256,128]{2,1,0:T(8,128)(2,1)} %get-tuple-element.26), channel_id=1, source_target_pairs={{0,8},{1,9},{2,10},{3,11},{4,12},{5,13},{6,14},{7,15},{8,0},{9,1},... | collective-permute-start | bytes 393224 | tf_op jit(solution)/shard_map/ppermute | solution.py:35
  7.2 0.1 collective-permute-start.3
  7.3 1.3 %collective-permute-start.4 = (bf16[2,256,128]{2,1,0:T(8,128)(2,1)}, bf16[2,256,128]{2,1,0:T(8,128)(2,1)S(1)}, u32[]{:S(2)}, u32[]{:S(2)}) collective-permute-start(bf16[2,256,128]{2,1,0:T(8,128)(2,1)} %get-tuple-element.28), channel_id=1, source_target_pairs={{0,4},{1,5},{2,6},{3,7},{4,0},{5,1},{6,2},{7,3},{8,12},{9,13},{10,... | collective-permute-start | bytes 393224 | tf_op jit(solution)/shard_map/ppermute | solution.py:35
  8.6 0.0 collective-permute-done.other_kv_ref
  8.6 1.2 %collective-permute-start.5 = (bf16[2,256,128]{2,1,0:T(8,128)(2,1)}, bf16[2,256,128]{2,1,0:T(8,128)(2,1)S(1)}, u32[]{:S(2)}, u32[]{:S(2)}) collective-permute-start(bf16[2,256,128]{2,1,0:T(8,128)(2,1)} %get-tuple-element.29), channel_id=1, source_target_pairs={{0,2},{1,3},{2,0},{3,1},{4,6},{5,7},{6,4},{7,5},{8,10},{9,11},{10,... | collective-permute-start | bytes 393224 | tf_op jit(solution)/shard_map/ppermute | solution.py:35
  9.9 0.0 copy-start
  9.9 1.2 %copy-done = bf16[1024,512]{1,0:T(8,128)(2,1)S(1)} copy-done((bf16[1024,512]{1,0:T(8,128)(2,1)S(1)}, bf16[1024,512]{1,0:T(8,128)(2,1)}, u32[]{:S(2)}) %copy-start) | copy-done | bytes 1048600
  11.1 1.0 %copy-done.2 = bf16[2,768,128]{2,1,0:T(8,128)(2,1)S(1)} copy-done((bf16[2,768,128]{2,1,0:T(8,128)(2,1)S(1)}, bf16[2,768,128]{2,1,0:T(8,128)(2,1)}, u32[]{:S(2)}) %copy-start.2) | copy-done | bytes 393240
  12.1 0.7 %copy-done.3 = s32[2,4,11]{2,1,0:T(4,128)S(1)} copy-done((s32[2,4,11]{2,1,0:T(4,128)S(1)}, s32[2,4,11]{2,1,0:T(4,128)}, u32[]{:S(2)}) %copy-start.3) | copy-done | bytes 376
  12.8 5.3 %stretch.1 = (f32[4,1024,128]{2,1,0:T(8,128)S(1)}, f32[4,1024,128]{2,1,0:T(8,128)S(1)}, f32[4,1024,128]{2,1,0:T(8,128)S(1)}, f32[8,128]{1,0:T(8,128)S(1)}, bf16[...) custom-call(s32[1]{0:T(128)} %bitcast.own_ref, s32[2,4,11]{2,1,0:T(4,128)S(1)} %copy-done.3, bf16[1024,512]{1,0:T(8,128)(2,1)S(1)} %copy-done, ...), custom_call_target="tpu_custom_call" | custom-call | flops 1000 | bytes 1000 | tf_op jit(solution)/shard_map/stretch/pallas_call | solution.py:351
  18.1 0.0 collective-permute-done.1.refs_0_
  18.1 1.7 %collective-permute-done.2.refs_1_ = bf16[2,256,128]{2,1,0:T(8,128)(2,1)S(1)} collective-permute-done((bf16[2,256,128]{2,1,0:T(8,128)(2,1)}, bf16[2,256,128]{2,1,0:T(8,128)(2,1)S(1)}, u32[]{:S(2)}, u32[]{:S(2)}) %collective-permute-start.2) | collective-permute-done | bytes 131104 | tf_op jit(solution)/shard_map/ppermute | solution.py:35
  19.8 0.0 collective-permute-done.3.refs_2_
  19.8 0.3 collective-permute-done.4.refs_3_
  20.1 0.0 collective-permute-done.5.refs_4_
  20.1 0.1 pack.2.refs_0_
  20.2 1.6 %collective-permute-start.6 = (bf16[6,2,256,128]{3,2,1,0:T(8,128)(2,1)S(1)}, bf16[6,2,256,128]{3,2,1,0:T(8,128)(2,1)S(1)}, u32[]{:S(2)}, u32[]{:S(2)}) collective-permute-start(bf16[6,2,256,128]{3,2,1,0:T(8,128)(2,1)S(1)} %pack.2.refs_0_), channel_id=1, source_target_pairs={{0,1},{1,0},{2,3},{3,2},{4,5},{5,4},{6,7},{7,6},{8,9},{9,8},{10,11... | collective-permute-start | bytes 2359304 | tf_op jit(solution)/shard_map/ppermute | solution.py:35
  21.7 0.0 copy-done.5
  21.7 0.0 collective-permute-start.7
  21.7 0.0 copy-done.4
  21.7 4.2 %collective-permute-start.8 = (bf16[2,256,128]{2,1,0:T(8,128)(2,1)S(1)}, bf16[2,256,128]{2,1,0:T(8,128)(2,1)S(1)}, u32[]{:S(2)}, u32[]{:S(2)}) collective-permute-start(bf16[2,256,128]{2,1,0:T(8,128)(2,1)S(1)} %copy-done.4), channel_id=1, source_target_pairs={{0,12},{1,13},{2,14},{3,15},{4,8},{5,9},{6,10},{7,11},{8,4},{9,5},... | collective-permute-start | bytes 393224 | tf_op jit(solution)/shard_map/ppermute | solution.py:35
  26.0 0.0 collective-permute-done.6.refs_1_
  26.0 0.0 copy-done.1
  26.0 12.1 %pages.2 = (f32[4,1024,128]{2,1,0:T(8,128)S(1)}, f32[4,1024,128]{2,1,0:T(8,128)S(1)}, f32[4,1024,128]{2,1,0:T(8,128)S(1)}, f32[8,128]{1,0:T(8,128)S(1)}) custom-call(s32[15]{0:T(128)S(1)} %get-tuple-element.24.list_ref, bf16[1024,512]{1,0:T(8,128)(2,1)S(1)} %copy-done.1, ...), custom_call_target="tpu_custom_call", output_to_operand_aliasing={{0}: (4, {}), {1}: (5, {}), {2}: (6, {})} | custom-call | flops 1000 | bytes 1000 | tf_op jit(solution)/shard_map/pages/pallas_call | solution.py:320
  38.1 0.0 collective-permute-done.7.refs_0_
  38.1 0.0 collective-permute-done.8.refs_1_
  38.1 0.7 %collective-permute-start.9 = (bf16[2,2,256,128]{3,2,1,0:T(8,128)(2,1)S(1)}, bf16[2,2,256,128]{3,2,1,0:T(8,128)(2,1)S(1)}, u32[]{:S(2)}, u32[]{:S(2)}) collective-permute-start(bf16[2,2,256,128]{3,2,1,0:T(8,128)(2,1)S(1)} %pack.3.refs_2_), channel_id=1, source_target_pairs={{0,1},{1,0},{2,3},{3,2},{4,5},{5,4},{6,7},{7,6},{8,9},{9,8},{10,11... | collective-permute-start | bytes 786440 | tf_op jit(solution)/shard_map/ppermute | solution.py:35
  38.8 1.2 %collective-permute-done.9.refs_3_ = bf16[2,2,256,128]{3,2,1,0:T(8,128)(2,1)S(1)} collective-permute-done((bf16[2,2,256,128]{3,2,1,0:T(8,128)(2,1)S(1)}, bf16[2,2,256,128]{3,2,1,0:T(8,128)(2,1)S(1)}, u32[]{:S(2)}, u32[]{:S(2)}) %collective-permute-start.9) | collective-permute-done | bytes 262176 | tf_op jit(solution)/shard_map/ppermute | solution.py:35
  40.0 8.6 %pages.3 = bf16[1024,512]{1,0:T(8,128)(2,1)} custom-call(s32[15]{0:T(128)S(1)} %get-tuple-element.24.list_ref, bf16[1024,512]{1,0:T(8,128)(2,1)S(1)} %copy-done.1, bf16[6,2,256,128]{3,2,1,0:T(8,128)(2,1)S(1)} %pack.2.refs_0_, bf16[6,2,256,128]{3,2,1,0:T(8,128)(2,1)S(1)} %collective-permute-done.6.refs_1_, bf16[2,2,256,128]{3,2,1,0:T(8,128)(2,1)S(1)} %pack.3.refs_2_, ...), custom_call_target="tpu_custom_call" | custom-call | flops 1000 | bytes 1000 | tf_op jit(solution)/shard_map/pages/pallas_call | solution.py:320
  (6 shorter events, 0.0 us)
Async XLA Ops:
  3.1 5.5 %collective-permute-start = (bf16[2,768,128]{2,1,0:T(8,128)(2,1)}, bf16[2,768,128]{2,1,0:T(8,128)(2,1)S(1)}, u32[]{:S(2)}, u32[]{:S(2)}) collective-permute-start(bf16[2,768,128]{2,1,0:T(8,128)(2,1)} %get-tuple-element.23.own_kv_ref), channel_id=1, source_target_pairs={{0,1},{1,0},{2,3},{3,2},{4,5},{5,4},{6,7},{7,6},{8,9},{9,8},{10,11... | collective-permute-start | bytes 1179656 | tf_op jit(solution)/shard_map/ppermute | solution.py:35
  3.9 14.2 %collective-permute-start.1 = (bf16[2,256,128]{2,1,0:T(8,128)(2,1)}, bf16[2,256,128]{2,1,0:T(8,128)(2,1)S(1)}, u32[]{:S(2)}, u32[]{:S(2)}) collective-permute-start(bf16[2,256,128]{2,1,0:T(8,128)(2,1)} %get-tuple-element.25), channel_id=1, source_target_pairs={{0,10},{1,11},{2,8},{3,9},{4,14},{5,15},{6,12},{7,13},{8,2},{9,3},... | collective-permute-start | bytes 393224 | tf_op jit(solution)/shard_map/ppermute | solution.py:35
  4.9 14.9 %collective-permute-start.2 = (bf16[2,256,128]{2,1,0:T(8,128)(2,1)}, bf16[2,256,128]{2,1,0:T(8,128)(2,1)S(1)}, u32[]{:S(2)}, u32[]{:S(2)}) collective-permute-start(bf16[2,256,128]{2,1,0:T(8,128)(2,1)} %get-tuple-element.26), channel_id=1, source_target_pairs={{0,8},{1,9},{2,10},{3,11},{4,12},{5,13},{6,14},{7,15},{8,0},{9,1},... | collective-permute-start | bytes 393224 | tf_op jit(solution)/shard_map/ppermute | solution.py:35
  7.2 12.6 %collective-permute-start.3 = (bf16[2,256,128]{2,1,0:T(8,128)(2,1)}, bf16[2,256,128]{2,1,0:T(8,128)(2,1)S(1)}, u32[]{:S(2)}, u32[]{:S(2)}) collective-permute-start(bf16[2,256,128]{2,1,0:T(8,128)(2,1)} %get-tuple-element.27), channel_id=1, source_target_pairs={{0,6},{1,7},{2,4},{3,5},{4,2},{5,3},{6,0},{7,1},{8,14},{9,15},{10,... | collective-permute-start | bytes 393224 | tf_op jit(solution)/shard_map/ppermute | solution.py:35
  7.3 12.8 %collective-permute-start.4 = (bf16[2,256,128]{2,1,0:T(8,128)(2,1)}, bf16[2,256,128]{2,1,0:T(8,128)(2,1)S(1)}, u32[]{:S(2)}, u32[]{:S(2)}) collective-permute-start(bf16[2,256,128]{2,1,0:T(8,128)(2,1)} %get-tuple-element.28), channel_id=1, source_target_pairs={{0,4},{1,5},{2,6},{3,7},{4,0},{5,1},{6,2},{7,3},{8,12},{9,13},{10,... | collective-permute-start | bytes 393224 | tf_op jit(solution)/shard_map/ppermute | solution.py:35
  8.6 11.5 %collective-permute-start.5 = (bf16[2,256,128]{2,1,0:T(8,128)(2,1)}, bf16[2,256,128]{2,1,0:T(8,128)(2,1)S(1)}, u32[]{:S(2)}, u32[]{:S(2)}) collective-permute-start(bf16[2,256,128]{2,1,0:T(8,128)(2,1)} %get-tuple-element.29), channel_id=1, source_target_pairs={{0,2},{1,3},{2,0},{3,1},{4,6},{5,7},{6,4},{7,5},{8,10},{9,11},{10,... | collective-permute-start | bytes 393224 | tf_op jit(solution)/shard_map/ppermute | solution.py:35
  9.9 1.2 %copy-start = (bf16[1024,512]{1,0:T(8,128)(2,1)S(1)}, bf16[1024,512]{1,0:T(8,128)(2,1)}, u32[]{:S(2)}) copy-start(bf16[1024,512]{1,0:T(8,128)(2,1)} %q_ref.5) | copy-start | bytes 3145732
  11.1 1.0 %copy-start.2 = (bf16[2,768,128]{2,1,0:T(8,128)(2,1)S(1)}, bf16[2,768,128]{2,1,0:T(8,128)(2,1)}, u32[]{:S(2)}) copy-start(bf16[2,768,128]{2,1,0:T(8,128)(2,1)} %get-tuple-element.23.own_kv_ref) | copy-start | bytes 1179652
  12.1 0.7 %copy-start.3 = (s32[2,4,11]{2,1,0:T(4,128)S(1)}, s32[2,4,11]{2,1,0:T(4,128)}, u32[]{:S(2)}) copy-start(s32[2,4,11]{2,1,0:T(4,128)} %table_ref.3) | copy-start | bytes 1060
  12.8 9.0 %copy-start.5 = (bf16[2,256,128]{2,1,0:T(8,128)(2,1)S(1)}, bf16[2,256,128]{2,1,0:T(8,128)(2,1)}, u32[]{:S(2)}) copy-start(bf16[2,256,128]{2,1,0:T(8,128)(2,1)} %get-tuple-element.32) | copy-start | bytes 393220
  12.8 9.0 %copy-start.4 = (bf16[2,256,128]{2,1,0:T(8,128)(2,1)S(1)}, bf16[2,256,128]{2,1,0:T(8,128)(2,1)}, u32[]{:S(2)}) copy-start(bf16[2,256,128]{2,1,0:T(8,128)(2,1)} %get-tuple-element.33) | copy-start | bytes 393220
  12.8 13.2 %copy-start.1 = (bf16[1024,512]{1,0:T(8,128)(2,1)S(1)}, bf16[1024,512]{1,0:T(8,128)(2,1)}, u32[]{:S(2)}) copy-start(bf16[1024,512]{1,0:T(8,128)(2,1)} %q_ref.5) | copy-start | bytes 3145732
  20.2 5.8 %collective-permute-start.6 = (bf16[6,2,256,128]{3,2,1,0:T(8,128)(2,1)S(1)}, bf16[6,2,256,128]{3,2,1,0:T(8,128)(2,1)S(1)}, u32[]{:S(2)}, u32[]{:S(2)}) collective-permute-start(bf16[6,2,256,128]{3,2,1,0:T(8,128)(2,1)S(1)} %pack.2.refs_0_), channel_id=1, source_target_pairs={{0,1},{1,0},{2,3},{3,2},{4,5},{5,4},{6,7},{7,6},{8,9},{9,8},{10,11... | collective-permute-start | bytes 2359304 | tf_op jit(solution)/shard_map/ppermute | solution.py:35
  21.7 16.4 %collective-permute-start.7 = (bf16[2,256,128]{2,1,0:T(8,128)(2,1)S(1)}, bf16[2,256,128]{2,1,0:T(8,128)(2,1)S(1)}, u32[]{:S(2)}, u32[]{:S(2)}) collective-permute-start(bf16[2,256,128]{2,1,0:T(8,128)(2,1)S(1)} %copy-done.5), channel_id=1, source_target_pairs={{0,14},{1,15},{2,12},{3,13},{4,10},{5,11},{6,8},{7,9},{8,6},{9,7},... | collective-permute-start | bytes 393224 | tf_op jit(solution)/shard_map/ppermute | solution.py:35
  21.7 16.4 %collective-permute-start.8 = (bf16[2,256,128]{2,1,0:T(8,128)(2,1)S(1)}, bf16[2,256,128]{2,1,0:T(8,128)(2,1)S(1)}, u32[]{:S(2)}, u32[]{:S(2)}) collective-permute-start(bf16[2,256,128]{2,1,0:T(8,128)(2,1)S(1)} %copy-done.4), channel_id=1, source_target_pairs={{0,12},{1,13},{2,14},{3,15},{4,8},{5,9},{6,10},{7,11},{8,4},{9,5},... | collective-permute-start | bytes 393224 | tf_op jit(solution)/shard_map/ppermute | solution.py:35
  38.1 1.9 %collective-permute-start.9 = (bf16[2,2,256,128]{3,2,1,0:T(8,128)(2,1)S(1)}, bf16[2,2,256,128]{3,2,1,0:T(8,128)(2,1)S(1)}, u32[]{:S(2)}, u32[]{:S(2)}) collective-permute-start(bf16[2,2,256,128]{3,2,1,0:T(8,128)(2,1)S(1)} %pack.3.refs_2_), channel_id=1, source_target_pairs={{0,1},{1,0},{2,3},{3,2},{4,5},{5,4},{6,7},{7,6},{8,9},{9,8},{10,11... | collective-permute-start | bytes 786440 | tf_op jit(solution)/shard_map/ppermute | solution.py:35
